TPU v7x, 32 devices: a whole 2x2x4 slice. The times are simulated.
32 devices in a mesh: dp: 16 (over z, y, x), fsdp: 2 (over core).
Axes of the slice: x: 2, y: 2, z: 4, core: 2. Of those that a mesh axis runs over, the one named last changes fastest.
Arguments:
- tokens: bfloat16 [4, 32, 128, 576], P(None, ('dp', 'fsdp')), may hold values from -6 to 6
- cotangent: bfloat16 [4, 32, 128, 576], P(None, ('dp', 'fsdp')), may hold values from -6 to 6
- lengths: int32 [4, 32, 4], P(None, ('dp', 'fsdp')), may hold values from 0 to 128, as said below
- w_query: bfloat16 [576, 576], P('fsdp'), may hold values from -0.25 to 0.25
- w_key: bfloat16 [576, 192], P('fsdp'), may hold values from -0.25 to 0.25
- w_value: bfloat16 [576, 192], P('fsdp'), may hold values from -0.25 to 0.25
- w_out: bfloat16 [576, 576], P('fsdp'), may hold values from -1 to 1
- w_gate: bfloat16 [576, 1536], P('fsdp'), may hold values from -0.25 to 0.25
- w_up: bfloat16 [576, 1536], P('fsdp'), may hold values from -0.25 to 0.25
- w_down: bfloat16 [1536, 576], P('fsdp'), may hold values from -0.15625 to 0.15625
- gain_attn: bfloat16 [576], P('fsdp'), may hold values from 0.5 to 1.5
- gain_ffn: bfloat16 [576], P('fsdp'), may hold values from 0.5 to 1.5
Outputs:
- output: bfloat16 [4, 32, 128, 576], P(None, ('dp', 'fsdp'))
- input_grad: float32 [4, 32, 128, 576], P(None, ('dp', 'fsdp'))
- grad_query: float32 [576, 576], P('fsdp')
- grad_key: float32 [576, 192], P('fsdp')
- grad_value: float32 [576, 192], P('fsdp')
- grad_out: float32 [576, 576], P('fsdp')
- grad_gate: float32 [576, 1536], P('fsdp')
- grad_up: float32 [576, 1536], P('fsdp')
- grad_down: float32 [1536, 576], P('fsdp')
- grad_gain_attn: float32 [576], P('fsdp')
- grad_gain_ffn: float32 [576], P('fsdp')
Inputs may be any that keep to these rules, and one draw needn't show every extreme that they name: lengths[m, b] lists the sequences packed in order from the start of bucket b of micro-batch m; zeros are empty slots; a row sums to at most 128 and the rest of the bucket is padding. Row [0, 0] is one sequence that fills its bucket.
All inputs are finite; a program needn't handle non-finite values.
Results may differ from a plain program's by a relative error of at most 0.022.
Values may be sent and summed in bfloat16 or wider, within the bound.
A program may use at most 192 MiB of HBM per device.

v0:
```python
import functools
import math

import jax
import jax.numpy as jnp
import ml_dtypes
import numpy as np
from jax import lax
from jax.experimental import pallas as pl
from jax.experimental.pallas import tpu as pltpu
from jax.sharding import PartitionSpec as P

HEADS = 9
KV_HEADS = 3
GROUP = HEADS // KV_HEADS
HD = 64
D = 576
FF = 1536
KVW = KV_HEADS * HD
BUCKET = 128
MESH = pl.DeviceIdType.MESH
F32 = jnp.float32
BF16 = jnp.bfloat16

WAVES = 4
STREAMS = 3
TILES = 4 * STREAMS
TILE_ROWS = 288
QKV = 1024
CHUNK = 256
ATTEND = 6


def nn(a, b):
    return lax.dot_general(a, b, (((1,), (0,)), ((), ())), preferred_element_type=F32)


def nt(a, b):
    return lax.dot_general(a, b, (((1,), (1,)), ((), ())), preferred_element_type=F32)


def tn(a, b):
    return lax.dot_general(a, b, (((0,), (0,)), ((), ())), preferred_element_type=F32)


def rope_table():
    inverse = np.exp(np.arange(HD // 2) * (-2.0 * math.log(10000.0) / HD))
    angles = inverse[:, None] * np.arange(BUCKET)[None, :]
    rest = np.concatenate([np.cos(angles), np.sin(angles)], axis=0)
    parts = []
    for unused in range(3):
        part = rest.astype(ml_dtypes.bfloat16)
        parts.append(part)
        rest = rest - part.astype(np.float64)
    return np.concatenate(parts, axis=0)


def stream_bits(wave, stream):
    if stream == 0:
        return (0, 1, 2)
    if stream == 1:
        return (1, 0, 2)
    return (2, 0, 1) if wave % 2 == 0 else (2, 1, 0)


TILE_TIME, STEP_TIME, WAVE_TIME, WAVE_STEP_TIME = 1.61, 2.4, 1.6, 1.6
SLACK = 1.0
PARTS = (
    ("down", 2.1, 0), ("gated", 1.7, None), ("gate", 2.1, 1), ("up", 2.1, 2), ("ffn", 2.1, None),
    ("norm_two", 0.75, None), ("branch", 0.7, None), ("scores_a", 1.0, None), ("scores_b", 1.0, None),
    ("qkv", 0.85, None), ("norm_one", 0.75, None), ("rest", 2.4, 3),
)


def plan_steps(bits):
    last = bits + 3
    free = {"core": 0.0, 0: 0.0, 1: 0.0, 2: 0.0, "far": 0.0}
    came, following, plan, now = {}, {}, {}, 0.0

    def send(w, s, k):
        b1, b2, b3 = stream_bits(w, s)
        links = {0: (b1, 2), 1: (b2, 1), 2: (b3, 0.5), bits: (b3, 0.5), bits + 1: (b2, 1), bits + 2: (b1, 2)}
        link, tiles = links.get(k, ("far", 0.5))
        time = tiles * TILE_TIME
        if link == "far":
            begin = max(now, free[2])
            free[2] = begin + time
            free["far"] = max(begin, free["far"]) + 2 * time
            came[w, s, k] = free["far"] + STEP_TIME + 0.6
        else:
            free[link] = max(now, free[link]) + time
            came[w, s, k] = free[link] + STEP_TIME

    def earliest():
        waiting = [(came[w] if k == 0 else came[w, s, k - 1], w, s, k) for (w, s), k in following.items() if k <= last]
        return min(waiting, default=None)

    for name, time, wave in PARTS + (("end", 0.0, None),):
        now += time
        steps = plan[name] = []
        if wave is not None:
            free["core"] = max(now, free["core"]) + WAVE_TIME
            came[wave] = free["core"] + WAVE_STEP_TIME
            following.update({(wave, s): 0 for s in range(STREAMS)})
        event = earliest()
        while event is not None and (name == "end" or event[0] <= now + SLACK):
            arrival, w, s, k = event
            now = max(now, arrival) + 0.08
            if k < last:
                send(w, s, k)
            following[w, s] = k + 1
            steps.append((w, s, k))
            event = earliest()
    return plan


def remote(src, dst, send, recv, target):
    return pltpu.make_async_remote_copy(
        src_ref=src, dst_ref=dst, send_sem=send, recv_sem=recv, device_id=target,
        device_id_type=MESH,
    )


class Reduction:
    def __init__(self, bits, dp, core, packed, res, ins, gain_buf, sems):
        self.bits, self.core, self.packed, self.res = bits, core, packed, res
        self.in1, self.in2, self.in3, self.in4 = ins
        self.gain_buf = gain_buf
        (
            self.half_send, self.half_recv, self.send_sem, self.recv_sem, self.gain_send, self.gain_recv,
        ) = sems
        self.value = [(dp // (1 << b)) % 2 for b in range(bits)]
        self.partner = [dp + (1 << b) * (1 - 2 * self.value[b]) for b in range(bits)]
        self.mate = (dp, 1 - core)
        self.targets = [self.mate] + [(self.partner[b], core) for b in range(bits)]
        self.last = bits + 3
        self.started, self.flight, self.halves, self.gain_copies = [], {}, {}, []
        self.plan, self.whole, self.whole_gains, self.count = plan_steps(bits), set(), set(), 0

    def start(self, copy):
        copy.start()
        self.started.append(copy)
        return copy

    def exchange(self, w):
        tiles = pl.ds(w * TILES, TILES)
        self.halves[w] = remote(
            self.packed.at[1 - self.core, tiles], self.res.at[tiles],
            self.half_send.at[w], self.half_recv.at[w], self.mate,
        )
        self.halves[w].start()

    def gain_start(self, i):
        target = self.targets[i]
        self.gain_copies.append(
            self.start(
                remote(
                    self.gain_buf.at[0, i], self.gain_buf.at[1, i], self.gain_send.at[i],
                    self.gain_recv.at[i], target,
                )
            )
        )

    def gain_finish(self, i):
        self.gain_copies[i].wait_recv()
        self.gain_buf[0, i + 1] = self.gain_buf[0, i] + self.gain_buf[1, i]

    def after(self, name):
        for part, unused, wave in PARTS:
            if part == name and wave is not None:
                self.exchange(wave)
        for w, s, step in self.plan[name]:
            if step == 0 and w not in self.whole:
                self.whole.add(w)
                self.halves[w].wait()
            self.stream_step(w, s, step)
            self.count += 1
            if name == "end" and self.count % 8 == 0:
                self.gain_step()

    def gain_step(self):
        i = len(self.gain_copies)
        if i > 0 and i not in self.whole_gains:
            self.gain_finish(i - 1)
            self.whole_gains.add(i)
        if i <= self.bits:
            self.gain_start(i)

    def stream_step(self, w, s, step):
        value, core, packed, res = self.value, self.core, self.packed, self.res
        b1, b2, b3 = stream_bits(w, s)
        base = w * TILES + 4 * s
        two = base + 2 * value[b1]
        one = two + value[b2]
        half = TILE_ROWS // 2
        rows = pl.ds(pl.multiple_of(half * value[b3], 16), half)
        slot = w * STREAMS + s

        def go(src, dst, bit):
            self.flight[(slot, step)] = self.start(
                remote(
                    src, dst, self.send_sem.at[slot, step], self.recv_sem.at[slot, step],
                    (self.partner[bit], core),
                )
            )

        if step > 0:
            self.flight[(slot, step - 1)].wait_recv()
        if step == 0:
            for t in range(4):
                packed[core, base + t] = (
                    packed[core, base + t].astype(F32) + res[base + t].astype(F32)
                ).astype(BF16)
            go(packed.at[core, pl.ds(base + 2 * (1 - value[b1]), 2)], self.in1.at[slot], b1)
        elif step == 1:
            for t in range(2):
                packed[core, two + t] = (
                    packed[core, two + t].astype(F32) + self.in1[slot, t].astype(F32)
                ).astype(BF16)
            go(packed.at[core, two + 1 - value[b2]], self.in2.at[slot], b2)
        elif step == 2:
            packed[core, one] = (
                packed[core, one].astype(F32) + self.in2[slot].astype(F32)
            ).astype(BF16)
            away = pl.ds(pl.multiple_of(half * (1 - value[b3]), 16), half)
            go(packed.at[core, one, away], self.in3.at[slot], b3)
        elif step < self.bits + 1:
            at = step - 3
            own = packed[core, one, rows] if at == 0 else self.in4[slot, 0, at - 1]
            came = self.in3[slot] if at == 0 else self.in4[slot, 1, at - 1]
            total = (own.astype(F32) + came.astype(F32)).astype(BF16)
            if step < self.bits:
                self.in4[slot, 0, at] = total
                go(self.in4.at[slot, 0, at], self.in4.at[slot, 1, at], step)
            else:
                res[one, rows] = total
                go(res.at[one, rows], res.at[one, rows], b3)
        elif step == self.bits + 1:
            go(res.at[one], res.at[one], b2)
        elif step == self.bits + 2:
            go(res.at[pl.ds(two, 2)], res.at[pl.ds(two, 2)], b1)


def layer_kernel(
    bits, buckets,
    lengths_ref, tokens_ref, cot_ref, wq_ref, wk_ref, wv_ref, wo_ref, wg_ref, wu_ref, wd_ref, ga_ref, gf_ref, table_ref,
    out_ref, dx_ref, res_ref, gain_out_ref,
    wqkv, wo, wg, wu, wd, gain_in, gain_own, gain, gain_sum, cs, bias,
    norm_one, norm_two, att, d_down, d_branch, qkv, probs, x_two, middle, hidden, d_up, d_gate,
    dn, d_att, d_qkv, packed, in1, in2, in3, in4, gain_buf,
    w_send, w_recv, w_local, half_send, half_recv, send_sem, recv_sem, gain_send, gain_recv,
):
    dp = lax.axis_index("dp")
    core = lax.axis_index("fsdp")
    total = buckets * BUCKET
    red = Reduction(
        bits, dp, core, packed, res_ref, (in1, in2, in3, in4), gain_buf,
        (half_send, half_recv, send_sem, recv_sem, gain_send, gain_recv),
    )
    barrier = pltpu.get_barrier_semaphore()
    for target in red.targets:
        pl.semaphore_signal(barrier, inc=1, device_id=target, device_id_type=MESH)

    scale = 1.0 / math.sqrt(HD)
    half = pl.ds(pl.multiple_of(core * TILE_ROWS, 16), TILE_ROWS)
    down_half = pl.ds(pl.multiple_of(core * (FF // 2), 128), FF // 2)
    wqkv[half, :] = jnp.concatenate(
        [
            (wq_ref[...].astype(F32) * scale).astype(BF16),
            wk_ref[...],
            wv_ref[...],
            jnp.zeros((TILE_ROWS, QKV - D - 2 * KVW), BF16),
        ],
        axis=1,
    )
    gain_own[0:1, :TILE_ROWS] = ga_ref[...].astype(F32).reshape(1, TILE_ROWS)
    gain_own[1:2, :TILE_ROWS] = gf_ref[...].astype(F32).reshape(1, TILE_ROWS)
    pl.semaphore_wait(barrier, len(red.targets))

    whole = [
        (wqkv.at[half], wqkv.at[half]), (wo_ref, wo.at[half]), (wg_ref, wg.at[half]),
        (wu_ref, wu.at[half]), (wd_ref, wd.at[:, down_half]), (gain_own, gain_in),
    ]
    arrivals, locals_ = {}, []
    for i in (5, 0, 1, 2, 3, 4):
        src, dst = whole[i]
        arrivals[i] = red.start(remote(src, dst, w_send.at[i], w_recv.at[i], red.mate))
        if 1 <= i <= 4:
            copy = pltpu.make_async_copy(src, dst, w_local.at[i - 1])
            copy.start()
            locals_.append(copy)

    def weight(i):
        if i >= 1:
            locals_[i - 1].wait()
        arrivals[i].wait_recv()

    def lanes(b):
        return slice(b * BUCKET, (b + 1) * BUCKET)

    place = lax.broadcasted_iota(jnp.int32, (BUCKET, BUCKET), 1)
    other = lax.broadcasted_iota(jnp.int32, (BUCKET, BUCKET), 0)
    alive = []
    for b in range(buckets):
        begin = jnp.zeros((BUCKET, BUCKET), jnp.int32)
        bound = 0
        for j in range(lengths_ref.shape[1]):
            bound = bound + lengths_ref[b, j]
            begin = begin + jnp.where(place >= bound, lengths_ref[b, j], 0)
        pick = jnp.where(place - begin == other, 1.0, 0.0).astype(BF16)
        parts = nn(table_ref[...], pick)
        cs[:, lanes(b)] = parts[:HD] + parts[HD : 2 * HD] + parts[2 * HD :]
        bias[b] = jnp.where((other >= begin) & (other <= place), 0.0, -1e30)
        alive.append((place[:1] < bound).astype(F32))

    d_qkv[D + 2 * KVW :, :] = jnp.zeros((QKV - D - 2 * KVW, 2 * total), BF16)
    gain_sum[...] = jnp.zeros_like(gain_sum)
    gain_buf[0, 0] = jnp.zeros(gain_buf.shape[2:], F32)
    arrivals[5].wait_recv()
    wide = lax.broadcasted_iota(jnp.int32, (8, 640), 1)
    low_half = jnp.where(core == 0, gain_own[...], gain_in[...])
    high_half = jnp.where(core == 0, gain_in[...], gain_own[...])
    gains = jnp.where(wide < TILE_ROWS, low_half, pltpu.roll(high_half, TILE_ROWS, 1))
    for i in range(2):
        gain[i] = jnp.broadcast_to(gains[i : i + 1, :D], (BUCKET, D)).T

    def x_of(p, b, rows=slice(None)):
        if p == 0:
            return tokens_ref[b, rows, :].astype(F32)
        return x_two[rows, lanes(b)]

    def middle_of(p, b, rows=slice(None)):
        return middle[p, rows, lanes(b)]

    def norm_forward(p, read, i, dst):
        for b in range(buckets):
            x = read(p, b)
            inv = lax.rsqrt(jnp.sum(x * x, axis=0, keepdims=True) * (1.0 / D) + 1e-05)
            dst[:, lanes(p * buckets + b)] = (x * inv * gain[i]).astype(BF16)

    def norm_backward(p, read, i, low_to):
        block = 64
        stats = []
        for b in range(buckets):
            squares = jnp.zeros((8, BUCKET), F32)
            dots = jnp.zeros((8, BUCKET), F32)
            for k in range(0, D, block):
                rows = slice(k, k + block)
                x = read(p, b, rows)
                d = dn[rows, lanes(b)] * gain[i, rows, :]
                squares = squares + jnp.sum((x * x).reshape(block // 8, 8, BUCKET), axis=0)
                dots = dots + jnp.sum((d * x).reshape(block // 8, 8, BUCKET), axis=0)
            inv = lax.rsqrt(jnp.sum(squares, axis=0, keepdims=True) * (1.0 / D) + 1e-05)
            mean = jnp.sum(dots, axis=0, keepdims=True) * inv * (1.0 / D)
            stats.append((inv, mean))
        for k in range(0, D, block):
            rows = slice(k, k + block)
            gain_term = gain_sum[i, rows, :]
            for b in range(buckets):
                inv, mean = stats[b]
                hat = read(p, b, rows) * inv
                d = dn[rows, lanes(b)]
                gain_term = gain_term + d * hat
                new = dx_ref[b, rows, :] + inv * (d * gain[i, rows, :] - hat * mean)
                dx_ref[b, rows, :] = new
                if low_to is not None:
                    low_to[rows, lanes(b)] = new.astype(BF16)
            gain_sum[i, rows, :] = gain_term

    def rope(z, b, sign):
        first, second = z[: HD // 2], z[HD // 2 :]
        cosines, sines = cs[: HD // 2, lanes(b)], cs[HD // 2 :, lanes(b)]
        if sign < 0:
            return jnp.concatenate([first * cosines + second * sines, second * cosines - first * sines], axis=0)
        return jnp.concatenate([first * cosines - second * sines, second * cosines + first * sines], axis=0)

    def head(h):
        return slice(HD * h, HD * (h + 1))

    def key_head(g):
        return head(HEADS + g)

    def value_head(g):
        return head(HEADS + KV_HEADS + g)

    def three(ref, g, where):
        return jnp.concatenate([ref[head(h), where] for h in range(GROUP * g, GROUP * (g + 1))], axis=1)

    def forward(p):
        at = slice(p * total, (p + 1) * total)
        norm_forward(p, x_of, 0, norm_one)
        if p == 0:
            weight(0)
        z = tn(wqkv[:, : D + 2 * KVW], norm_one[:, at])
        for h in range(HEADS + KV_HEADS):
            for b in range(buckets):
                qkv[head(h), lanes(p * buckets + b)] = rope(z[head(h), lanes(b)], b, 1).astype(BF16)
        qkv[D + KVW :, at] = z[D + KVW :].astype(BF16)
        todo = [(b, g) for b in range(buckets) for g in range(KV_HEADS)]
        for first in range(0, len(todo), ATTEND):
            part = [(b, g, lanes(p * buckets + b)) for b, g in todo[first : first + ATTEND]]
            scores = [
                tn(qkv[key_head(g), here], three(qkv, g, here)) + jnp.concatenate([bias[b]] * GROUP, axis=1)
                for b, g, here in part
            ]
            lows = []
            for (b, g, here), score in zip(part, scores):
                e = jnp.exp(score - jnp.max(score, axis=0, keepdims=True))
                low = (e * (1.0 / jnp.sum(e, axis=0, keepdims=True))).astype(BF16)
                probs[p * buckets + b, g] = low
                lows.append(low)
            for (b, g, here), low in zip(part, lows):
                mixed = nn(qkv[value_head(g), here], low).astype(BF16)
                for i in range(GROUP):
                    att[head(GROUP * g + i), here] = mixed[:, lanes(i)]
        if p == 0:
            weight(1)
        mixed = tn(wo[...], att[:, at])
        for b in range(buckets):
            middle[p, :, lanes(b)] = x_of(p, b) + mixed[:, lanes(b)]
        norm_forward(p, middle_of, 1, norm_two)
        if p == 0:
            weight(2)
            weight(3)
        for c in range(0, FF, CHUNK):
            rows = slice(c, c + CHUNK)
            gate = tn(wg[:, rows], norm_two[:, at])
            up = tn(wu[:, rows], norm_two[:, at])
            s = 1.0 / (1.0 + jnp.exp(-gate))
            silu = gate * s
            hidden[rows, at] = (silu * up).astype(BF16)
            d_up[rows, at] = silu.astype(BF16)
            d_gate[rows, at] = (up * (s + silu * (1.0 - s))).astype(BF16)
        if p == 0:
            weight(4)
        result = middle[p] + nn(wd[...], hidden[:, at])
        if p == 0:
            x_two[...] = result
        else:
            for b in range(buckets):
                out_ref[b] = (result[:, lanes(b)] * alive[b]).astype(BF16)
                grad = cot_ref[b].astype(F32) * alive[b]
                dx_ref[b] = grad
                d_down[:, lanes(buckets + b)] = grad.astype(BF16)

    def put(first, block):
        low = block.astype(BF16)
        for h in range(2):
            for j in range(2):
                packed[h, first + j] = low[TILE_ROWS * h : TILE_ROWS * (h + 1), 128 * j : 128 * (j + 1)]

    def grad_down():
        per = FF // 2 // CHUNK
        for c in range(FF // CHUNK):
            low = nt(d_down[...], hidden[c * CHUNK : (c + 1) * CHUNK, :]).astype(BF16)
            for h in range(2):
                for j in range(2):
                    packed[c // per, 6 * h + 2 * (c % per) + j] = low[
                        TILE_ROWS * h : TILE_ROWS * (h + 1), 128 * j : 128 * (j + 1)
                    ]

    def grad_ffn(wave, d):
        for c in range(FF // CHUNK):
            put(wave * TILES + 2 * c, nt(norm_two[...], d[c * CHUNK : (c + 1) * CHUNK, :]))

    def backward(p):
        at = slice(p * total, (p + 1) * total)
        if p == 0:
            grad_down()
            red.after("down")
        for c in range(0, FF, CHUNK):
            rows = slice(c, c + CHUNK)
            d_hidden = tn(wd[:, rows], d_down[:, at])
            d_up[rows, at] = (d_hidden * d_up[rows, at].astype(F32)).astype(BF16)
            d_gate[rows, at] = (d_hidden * d_gate[rows, at].astype(F32)).astype(BF16)
        if p == 0:
            red.after("gated")
            grad_ffn(1, d_gate)
            red.after("gate")
            grad_ffn(2, d_up)
            red.after("up")
        dn[...] = nn(wg[...], d_gate[:, at]) + nn(wu[...], d_up[:, at])
        if p == 0:
            red.after("ffn")
        norm_backward(p, middle_of, 1, d_branch.at[:, at])
        if p == 0:
            red.after("norm_two")
        d_att[...] = nn(wo[...], d_branch[:, at]).astype(BF16)
        if p == 0:
            red.after("branch")
        todo = [(b, g) for b in range(buckets) for g in range(KV_HEADS)]
        for first in range(0, len(todo), ATTEND):
            part = todo[first : first + ATTEND]
            d_probs = [
                tn(qkv[value_head(g), lanes(p * buckets + b)], three(d_att, g, lanes(b))) for b, g in part
            ]
            d_scores = []
            for (b, g), d in zip(part, d_probs):
                pr = probs[p * buckets + b, g].astype(F32)
                d_scores.append((pr * (d - jnp.sum(d * pr, axis=0, keepdims=True))).astype(BF16))
            for (b, g), ds in zip(part, d_scores):
                here = lanes(p * buckets + b)
                d_query = nn(qkv[key_head(g), here], ds)
                for i in range(GROUP):
                    d_qkv[head(GROUP * g + i), here] = rope(d_query[:, lanes(i)], b, -1).astype(BF16)
                d_qkv[key_head(g), here] = rope(nt(three(qkv, g, here), ds), b, -1).astype(BF16)
                d_qkv[value_head(g), here] = nt(
                    three(d_att, g, lanes(b)), probs[p * buckets + b, g]
                ).astype(BF16)
            if p == 0:
                red.after("scores_a" if first == 0 else "scores_b")
        dn[...] = nn(wqkv[...], d_qkv[:, at])
        if p == 0:
            red.after("qkv")
        norm_backward(p, x_of, 0, d_down.at[:, :total] if p == 1 else None)
        if p == 0:
            red.after("norm_one")

    forward(0)
    forward(1)
    backward(1)
    backward(0)
    for i in range(2):
        gain_buf[0, 0, i : i + 1, :D] = jnp.sum(gain_sum[i].T, axis=0, keepdims=True)
    red.gain_step()

    column = lax.broadcasted_iota(jnp.int32, (1, CHUNK), 1)
    for c in range(3):
        block = nt(norm_one[...], d_qkv[c * CHUNK : (c + 1) * CHUNK, :])
        put(3 * TILES + 2 * c, block * jnp.where(column + c * CHUNK < D, scale, 1.0))
    block = nt(norm_one[...], d_qkv[3 * CHUNK :, :])
    rest = nt(att[...], d_branch[2 * CHUNK :, :])
    put(3 * TILES + 6, jnp.concatenate([block[:, : D + 2 * KVW - 3 * CHUNK], rest], axis=1))
    for c in range(2):
        put(3 * TILES + 8 + 2 * c, nt(att[...], d_branch[c * CHUNK : (c + 1) * CHUNK, :]))
    red.after("rest")
    red.after("end")
    while len(red.whole_gains) <= bits:
        red.gain_step()
    sums = gain_buf[0, bits + 1]
    gain_out_ref[...] = jnp.where(core == 0, sums, pltpu.roll(sums, 640 - TILE_ROWS, 1))
    for copy in red.started:
        copy.wait_send()


def run_layer(bits, lengths, tokens, cotangent, weights, gains):
    buckets = tokens.shape[0]
    total = buckets * BUCKET
    slots = WAVES * STREAMS
    half = (TILE_ROWS // 2, 128)
    steps = bits + 3
    vmem = pl.BlockSpec(memory_space=pltpu.VMEM)
    hbm = pl.BlockSpec(memory_space=pl.ANY)
    dma = pltpu.SemaphoreType.DMA
    grads = (WAVES * TILES, TILE_ROWS, 128)
    scratch = [
        ((D, QKV), BF16), ((D, D), BF16), ((D, FF), BF16), ((D, FF), BF16), ((D, FF), BF16),
        ((8, 640), F32), ((8, 640), F32), ((2, D, BUCKET), F32), ((2, D, BUCKET), F32),
        ((HD, total), F32), ((buckets, BUCKET, BUCKET), F32),
        ((D, 2 * total), BF16), ((D, 2 * total), BF16), ((D, 2 * total), BF16),
        ((D, 2 * total), BF16), ((D, 2 * total), BF16),
        ((D + 2 * KVW, 2 * total), BF16),
        ((2 * buckets, KV_HEADS, BUCKET, GROUP * BUCKET), BF16),
        ((D, total), F32), ((2, D, total), F32),
        ((FF, 2 * total), BF16), ((FF, 2 * total), BF16), ((FF, 2 * total), BF16),
        ((D, total), F32), ((D, total), BF16), ((QKV, 2 * total), BF16),
        ((2, *grads), BF16), ((slots, 2, TILE_ROWS, 128), BF16), ((slots, TILE_ROWS, 128), BF16),
        ((slots, *half), BF16), ((slots, 2, bits - 3, *half), BF16), ((2, bits + 2, 8, 640), F32),
    ]
    return pl.pallas_call(
        functools.partial(layer_kernel, bits, buckets),
        out_shape=(
            jax.ShapeDtypeStruct((buckets, D, BUCKET), BF16),
            jax.ShapeDtypeStruct((buckets, D, BUCKET), F32),
            jax.ShapeDtypeStruct(grads, BF16),
            jax.ShapeDtypeStruct((8, 640), F32),
        ),
        in_specs=[pl.BlockSpec(memory_space=pltpu.SMEM)] + [vmem] * 5 + [hbm] * 4 + [vmem] * 3,
        out_specs=(vmem,) * 4,
        scratch_shapes=[pltpu.VMEM(shape, dtype) for shape, dtype in scratch]
        + [
            dma((6,)), dma((6,)), dma((4,)), dma((WAVES,)), dma((WAVES,)), dma((slots, steps)),
            dma((slots, steps)), dma((bits + 1,)), dma((bits + 1,)),
        ],
        compiler_params=pltpu.CompilerParams(
            collective_id=0, has_side_effects=True, vmem_limit_bytes=63 << 20
        ),
    )(lengths, tokens, cotangent, *weights, *gains, jnp.asarray(rope_table()))


def unpack_kernel(
    res_hbm, out_in, dx_in, gain_in,
    out_ref, dx_ref, gq, gk, gv, go, gg, gu, gd, ga, gf,
    res_ref, out_block, dx_block, query, key, value, branch, gate, up, down, in_sem, out_sem,
):
    arrivals = [
        pltpu.make_async_copy(res_hbm.at[pl.ds(w * TILES, TILES)], res_ref.at[pl.ds(w * TILES, TILES)], in_sem.at[w])
        for w in range(WAVES)
    ]
    arrivals.append(pltpu.make_async_copy(dx_in, dx_block, in_sem.at[WAVES]))
    arrivals.append(pltpu.make_async_copy(out_in, out_block, in_sem.at[WAVES + 1]))
    for copy in arrivals:
        copy.start()
    copies = []
    ga[...] = gain_in[0, :TILE_ROWS]
    gf[...] = gain_in[1, :TILE_ROWS]

    def tile(t):
        return res_ref[t].astype(F32)

    def leave(src, dst):
        copy = pltpu.make_async_copy(src, dst, out_sem.at[len(copies)])
        copy.start()
        copies.append(copy)

    arrivals[0].wait()
    for j in range(6):
        for h in range(2):
            down[TILE_ROWS * h : TILE_ROWS * (h + 1), 128 * j : 128 * (j + 1)] = tile(6 * h + j)
    leave(down, gd)
    for w, block, dst in ((1, gate, gg), (2, up, gu)):
        arrivals[w].wait()
        for j in range(TILES):
            block[:, 128 * j : 128 * (j + 1)] = tile(w * TILES + j)
        leave(block, dst)
    arrivals[3].wait()
    first = 3 * TILES
    for j in range(4):
        query[:, 128 * j : 128 * (j + 1)] = tile(first + j)
        branch[:, 128 * j : 128 * (j + 1)] = tile(first + 8 + j)
    shared, last = tile(first + 4), tile(first + 7)
    query[:, 512:] = shared[:, :64]
    leave(query, gq)
    branch[:, 512:] = last[:, 64:]
    leave(branch, go)
    key[...] = jnp.concatenate([shared[:, 64:], tile(first + 5)], axis=1)
    leave(key, gk)
    value[...] = jnp.concatenate([tile(first + 6), last[:, :64]], axis=1)
    leave(value, gv)
    arrivals[WAVES].wait()
    leave(dx_block, dx_ref)
    arrivals[WAVES + 1].wait()
    leave(out_block, out_ref)
    for copy in copies:
        copy.wait()


def unpack(res, output, input_grad, gain_sum):
    shapes = [
        (TILE_ROWS, D), (TILE_ROWS, KVW), (TILE_ROWS, KVW), (TILE_ROWS, D), (TILE_ROWS, FF), (TILE_ROWS, FF),
        (D, FF // 2),
    ]
    vmem = pl.BlockSpec(memory_space=pltpu.VMEM)
    hbm = pl.BlockSpec(memory_space=pl.ANY)
    dma = pltpu.SemaphoreType.DMA
    return pl.pallas_call(
        unpack_kernel,
        out_shape=(
            jax.ShapeDtypeStruct(output.shape, output.dtype),
            jax.ShapeDtypeStruct(input_grad.shape, input_grad.dtype),
            *(jax.ShapeDtypeStruct(shape, F32) for shape in shapes + [(TILE_ROWS,)] * 2),
        ),
        in_specs=[hbm] * 3 + [vmem],
        out_specs=(hbm,) * 9 + (vmem,) * 2,
        scratch_shapes=[pltpu.VMEM(a.shape, a.dtype) for a in (res, output, input_grad)]
        + [pltpu.VMEM(shape, F32) for shape in shapes]
        + [dma((WAVES + 2,)), dma((len(shapes) + 2,))],
        compiler_params=pltpu.CompilerParams(vmem_limit_bytes=63 << 20),
    )(res, output, input_grad, gain_sum)


def on_device(
    bits, tokens, cotangent, lengths, w_query, w_key, w_value, w_out, w_gate, w_up, w_down, gain_attn, gain_ffn,
):
    output, input_grad, res, gain_sum = run_layer(
        bits,
        lengths[:, 0],
        tokens[:, 0].transpose(0, 2, 1),
        cotangent[:, 0].transpose(0, 2, 1),
        (w_query, w_key, w_value, w_out, w_gate, w_up, w_down.T),
        (gain_attn, gain_ffn),
    )
    output, input_grad, gq, gk, gv, go, gg, gu, gd, ga, gf = unpack(res, output, input_grad, gain_sum)
    return (
        output.transpose(0, 2, 1)[:, None], input_grad.transpose(0, 2, 1)[:, None],
        gq, gk, gv, go, gg, gu, gd.T, ga, gf,
    )


def solution(mesh):
    rows = P(None, ("dp", "fsdp"), None, None)
    weight = P("fsdp", None)
    in_specs = (rows, rows, P(None, ("dp", "fsdp"), None)) + (weight,) * 7 + (P("fsdp"),) * 2
    out_specs = (rows, rows) + (weight,) * 7 + (P("fsdp"),) * 2
    bits = mesh.shape["dp"].bit_length() - 1
    return jax.shard_map(
        functools.partial(on_device, bits),
        mesh=mesh,
        in_specs=in_specs,
        out_specs=out_specs,
        check_vma=False,
    )
```

profile of v0, /device:TPU:0, one launch (start us, length us, event | category | flops | bytes accessed | tf_op | source)
XLA Modules:
  0.0 108.7 jit_solution(4733246404192851785)
XLA Ops:
  0.6 101.6 %shard_map.212 = (bf16[4,576,128]{2,1,0:T(8,128)(2,1)}, f32[4,576,128]{2,1,0:T(8,128)}, bf16[48,288,128]{2,1,0:T(8,128)(2,1)}, f32[8,640]{1,0:T(8,128)}) custom-call(s32[4,4]{1,0:T(4,128)} %bitcast.22, bf16[4,576,128]{2,1,0:T(8,128)(2,1)} %bitcast.20, bf16[4,576,128]{2,1,0:T(8,128)(2,1)} %bitcast.21, bf16[288,576]{1,0:T(8,128)(2,1)} %wq_ref.1, ...), custom_call_target="tpu_custom_call" | custom-call | tf_op jit(solution)/shard_map/pallas_call | solution.py:570
  102.2 6.3 %shard_map.213 = (bf16[4,576,128]{2,1,0:T(8,128)(2,1)}, f32[4,576,128]{2,1,0:T(8,128)}, f32[288,576]{1,0:T(8,128)}, f32[288,192]{1,0:T(8,128)}, f32[288,192]{1,0...) custom-call(bf16[48,288,128]{2,1,0:T(8,128)(2,1)} %get-tuple-element, ...), custom_call_target="tpu_custom_call" | custom-call | tf_op jit(solution)/shard_map/pallas_call | solution.py:656
where the time goes:
time: 109 us
  Pallas kernels  108 us (99%)
    pallas_call x1, Pallas kernels, run_layer(): pl.pallas_call(functools.partial(layer_kernel, bits, buckets), out_shape=...  102 us
    pallas_call x1, Pallas kernels, unpack(): pl.pallas_call(unpack_kernel, out_shape=(jax.ShapeDtypeStruct(output.shap...  6.25 us

commit v1 on v0

--- a/solution.py
+++ b/solution.py
@@ -55,29 +55,35 @@
     return np.concatenate(parts, axis=0)
 
 
+STREAM_BITS = (
+    ((1, 2, 0), (0, 1, 2), (2, 1, 0)),
+    ((1, 0, 2), (0, 2, 1), (2, 1, 0)),
+    ((0, 2, 1), (1, 0, 2), (2, 1, 0)),
+    ((2, 1, 0), (1, 0, 2), (0, 2, 1)),
+)
+
+
 def stream_bits(wave, stream):
-    if stream == 0:
-        return (0, 1, 2)
-    if stream == 1:
-        return (1, 0, 2)
-    return (2, 0, 1) if wave % 2 == 0 else (2, 1, 0)
-
-
-TILE_TIME, STEP_TIME, WAVE_TIME, WAVE_STEP_TIME = 1.61, 2.4, 1.6, 1.6
-SLACK = 1.0
+    return STREAM_BITS[wave][stream]
+
+
+TILE_TIME, STEP_TIME, WAVE_TIME, WAVE_STEP_TIME = 1.42, 2.65, 1.3, 1.5
+STEP_RANK, WAVE_RANK, THIRD_RANK = 6.404041155859943, 5.683458090508361, 0.024984608445357243
 PARTS = (
-    ("down", 2.1, 0), ("gated", 1.7, None), ("gate", 2.1, 1), ("up", 2.1, 2), ("ffn", 2.1, None),
-    ("norm_two", 0.75, None), ("branch", 0.7, None), ("scores_a", 1.0, None), ("scores_b", 1.0, None),
-    ("qkv", 0.85, None), ("norm_one", 0.75, None), ("rest", 2.4, 3),
+    ("down_a", 1.05, 0, 1.0), ("down_b", 1.05, None, 1.0), ("gated", 1.7, None, -1.0), ("gate_a", 1.05, None, -5.0),
+    ("gate_b", 1.05, 1, 0.0), ("up_a", 1.05, None, 1.0), ("up_b", 1.05, 2, 0.3), ("ffn", 2.1, None, 0.6),
+    ("norm_two", 0.75, None, -1.0), ("branch", 0.7, None, -5.0), ("scores_a", 1.0, None, 0.3),
+    ("scores_b", 1.0, None, 0.0), ("rest", 2.1, 3, 0.6), ("qkv", 0.85, None, 0.6), ("norm_one", 1.1, None, -1.0),
+    ("end", 0.0, None, 1e9),
 )
 
 
 def plan_steps(bits):
     last = bits + 3
     free = {"core": 0.0, 0: 0.0, 1: 0.0, 2: 0.0, "far": 0.0}
-    came, following, plan, now = {}, {}, {}, 0.0
-
-    def send(w, s, k):
+    waiting, plan, now = {}, {}, 0.0
+
+    def sent(w, s, k):
         b1, b2, b3 = stream_bits(w, s)
         links = {0: (b1, 2), 1: (b2, 1), 2: (b3, 0.5), bits: (b3, 0.5), bits + 1: (b2, 1), bits + 2: (b1, 2)}
         link, tiles = links.get(k, ("far", 0.5))
@@ -86,31 +92,32 @@
             begin = max(now, free[2])
             free[2] = begin + time
             free["far"] = max(begin, free["far"]) + 2 * time
-            came[w, s, k] = free["far"] + STEP_TIME + 0.6
-        else:
-            free[link] = max(now, free[link]) + time
-            came[w, s, k] = free[link] + STEP_TIME
-
-    def earliest():
-        waiting = [(came[w] if k == 0 else came[w, s, k - 1], w, s, k) for (w, s), k in following.items() if k <= last]
-        return min(waiting, default=None)
-
-    for name, time, wave in PARTS + (("end", 0.0, None),):
+            return free["far"] + STEP_TIME + 0.6
+        free[link] = max(now, free[link]) + time
+        return free[link] + STEP_TIME
+
+    for name, time, wave, slack in PARTS:
         now += time
+        limit = now + slack
         steps = plan[name] = []
         if wave is not None:
             free["core"] = max(now, free["core"]) + WAVE_TIME
-            came[wave] = free["core"] + WAVE_STEP_TIME
-            following.update({(wave, s): 0 for s in range(STREAMS)})
-        event = earliest()
-        while event is not None and (name == "end" or event[0] <= now + SLACK):
-            arrival, w, s, k = event
-            now = max(now, arrival) + 0.08
+            waiting.update({(wave, s): (free["core"] + WAVE_STEP_TIME, 0) for s in range(STREAMS)})
+        while True:
+            ranked = [
+                (max(came, now) + STEP_RANK * k + WAVE_RANK * w + THIRD_RANK * (s == 2), came, w, s, k)
+                for (w, s), (came, k) in waiting.items()
+                if came <= limit
+            ]
+            if not ranked:
+                break
+            unused, came, w, s, k = min(ranked)
+            now = max(now, came) + 0.2
+            steps.append((w, s, k))
             if k < last:
-                send(w, s, k)
-            following[w, s] = k + 1
-            steps.append((w, s, k))
-            event = earliest()
+                waiting[w, s] = (sent(w, s, k), k + 1)
+            else:
+                del waiting[w, s]
     return plan
 
 
@@ -122,19 +129,19 @@
 
 
 class Reduction:
-    def __init__(self, bits, dp, core, packed, res, ins, gain_buf, sems):
-        self.bits, self.core, self.packed, self.res = bits, core, packed, res
+    def __init__(self, bits, dp, core, packed, res, res_out, ins, gain_buf, sems):
+        self.bits, self.core, self.packed, self.res, self.res_out = bits, core, packed, res, res_out
         self.in1, self.in2, self.in3, self.in4 = ins
         self.gain_buf = gain_buf
         (
-            self.half_send, self.half_recv, self.send_sem, self.recv_sem, self.gain_send, self.gain_recv,
+            self.half_send, self.half_recv, self.send_sem, self.recv_sem, self.gain_send, self.gain_recv, self.res_sem,
         ) = sems
         self.value = [(dp // (1 << b)) % 2 for b in range(bits)]
         self.partner = [dp + (1 << b) * (1 - 2 * self.value[b]) for b in range(bits)]
         self.mate = (dp, 1 - core)
         self.targets = [self.mate] + [(self.partner[b], core) for b in range(bits)]
         self.last = bits + 3
-        self.started, self.flight, self.halves, self.gain_copies = [], {}, {}, []
+        self.started, self.flight, self.halves, self.gain_copies, self.leaving = [], {}, {}, [], []
         self.plan, self.whole, self.whole_gains, self.count = plan_steps(bits), set(), set(), 0
 
     def start(self, copy):
@@ -166,7 +173,7 @@
         self.gain_buf[0, i + 1] = self.gain_buf[0, i] + self.gain_buf[1, i]
 
     def after(self, name):
-        for part, unused, wave in PARTS:
+        for part, unused, wave, slack in PARTS:
             if part == name and wave is not None:
                 self.exchange(wave)
         for w, s, step in self.plan[name]:
@@ -239,27 +246,47 @@
             go(res.at[one], res.at[one], b2)
         elif step == self.bits + 2:
             go(res.at[pl.ds(two, 2)], res.at[pl.ds(two, 2)], b1)
+        else:
+            copy = pltpu.make_async_copy(
+                res.at[pl.ds(base, 4)], self.res_out.at[pl.ds(base, 4)], self.res_sem.at[slot]
+            )
+            copy.start()
+            self.leaving.append(copy)
 
 
 def layer_kernel(
     bits, buckets,
-    lengths_ref, tokens_ref, cot_ref, wq_ref, wk_ref, wv_ref, wo_ref, wg_ref, wu_ref, wd_ref, ga_ref, gf_ref, table_ref,
-    out_ref, dx_ref, res_ref, gain_out_ref,
+    lengths_ref, tokens_hbm, cot_hbm, wq_hbm, wk_hbm, wv_hbm, wo_ref, wg_ref, wu_ref, wd_ref, ga_ref, gf_ref, table_hbm,
+    out_hbm, dx_hbm, res_hbm, gain_out_ref,
+    tokens_ref, cot_ref, wq_ref, wk_ref, wv_ref, table_ref, out_ref, dx_ref, res_ref,
     wqkv, wo, wg, wu, wd, gain_in, gain_own, gain, gain_sum, cs, bias,
     norm_one, norm_two, att, d_down, d_branch, qkv, probs, x_two, middle, hidden, d_up, d_gate,
     dn, d_att, d_qkv, packed, in1, in2, in3, in4, gain_buf,
-    w_send, w_recv, w_local, half_send, half_recv, send_sem, recv_sem, gain_send, gain_recv,
+    w_send, w_recv, w_local, half_send, half_recv, send_sem, recv_sem, gain_send, gain_recv, res_sem, in_sem, out_sem,
 ):
     dp = lax.axis_index("dp")
     core = lax.axis_index("fsdp")
     total = buckets * BUCKET
     red = Reduction(
-        bits, dp, core, packed, res_ref, (in1, in2, in3, in4), gain_buf,
-        (half_send, half_recv, send_sem, recv_sem, gain_send, gain_recv),
+        bits, dp, core, packed, res_ref, res_hbm, (in1, in2, in3, in4), gain_buf,
+        (half_send, half_recv, send_sem, recv_sem, gain_send, gain_recv, res_sem),
     )
     barrier = pltpu.get_barrier_semaphore()
     for target in red.targets:
         pl.semaphore_signal(barrier, inc=1, device_id=target, device_id_type=MESH)
+    inputs = [
+        pltpu.make_async_copy(src, dst, in_sem.at[i])
+        for i, (src, dst) in enumerate(
+            [
+                (wq_hbm, wq_ref), (wk_hbm, wk_ref), (wv_hbm, wv_ref), (table_hbm, table_ref), (tokens_hbm, tokens_ref),
+                (cot_hbm, cot_ref),
+            ]
+        )
+    ]
+    for copy in inputs:
+        copy.start()
+    for copy in inputs[:3]:
+        copy.wait()
 
     scale = 1.0 / math.sqrt(HD)
     half = pl.ds(pl.multiple_of(core * TILE_ROWS, 16), TILE_ROWS)
@@ -301,6 +328,7 @@
     place = lax.broadcasted_iota(jnp.int32, (BUCKET, BUCKET), 1)
     other = lax.broadcasted_iota(jnp.int32, (BUCKET, BUCKET), 0)
     alive = []
+    inputs[3].wait()
     for b in range(buckets):
         begin = jnp.zeros((BUCKET, BUCKET), jnp.int32)
         bound = 0
@@ -313,6 +341,7 @@
         bias[b] = jnp.where((other >= begin) & (other <= place), 0.0, -1e30)
         alive.append((place[:1] < bound).astype(F32))
 
+    inputs[4].wait()
     d_qkv[D + 2 * KVW :, :] = jnp.zeros((QKV - D - 2 * KVW, 2 * total), BF16)
     gain_sum[...] = jnp.zeros_like(gain_sum)
     gain_buf[0, 0] = jnp.zeros(gain_buf.shape[2:], F32)
@@ -437,6 +466,7 @@
         if p == 0:
             x_two[...] = result
         else:
+            inputs[5].wait()
             for b in range(buckets):
                 out_ref[b] = (result[:, lanes(b)] * alive[b]).astype(BF16)
                 grad = cot_ref[b].astype(F32) * alive[b]
@@ -449,25 +479,26 @@
             for j in range(2):
                 packed[h, first + j] = low[TILE_ROWS * h : TILE_ROWS * (h + 1), 128 * j : 128 * (j + 1)]
 
-    def grad_down():
+    def grad_down(h):
         per = FF // 2 // CHUNK
-        for c in range(FF // CHUNK):
-            low = nt(d_down[...], hidden[c * CHUNK : (c + 1) * CHUNK, :]).astype(BF16)
-            for h in range(2):
+        for c in range(per):
+            rows = pl.ds(pl.multiple_of(h * (FF // 2) + c * CHUNK, CHUNK), CHUNK)
+            low = nt(d_down[...], hidden[rows, :]).astype(BF16)
+            for i in range(2):
                 for j in range(2):
-                    packed[c // per, 6 * h + 2 * (c % per) + j] = low[
-                        TILE_ROWS * h : TILE_ROWS * (h + 1), 128 * j : 128 * (j + 1)
-                    ]
-
-    def grad_ffn(wave, d):
-        for c in range(FF // CHUNK):
+                    packed[h, 6 * i + 2 * c + j] = low[TILE_ROWS * i : TILE_ROWS * (i + 1), 128 * j : 128 * (j + 1)]
+
+    def grad_ffn(wave, d, part):
+        for c in range(3 * part, 3 * part + 3):
             put(wave * TILES + 2 * c, nt(norm_two[...], d[c * CHUNK : (c + 1) * CHUNK, :]))
 
     def backward(p):
         at = slice(p * total, (p + 1) * total)
         if p == 0:
-            grad_down()
-            red.after("down")
+            grad_down(1 - core)
+            red.after("down_a")
+            grad_down(core)
+            red.after("down_b")
         for c in range(0, FF, CHUNK):
             rows = slice(c, c + CHUNK)
             d_hidden = tn(wd[:, rows], d_down[:, at])
@@ -475,10 +506,11 @@
             d_gate[rows, at] = (d_hidden * d_gate[rows, at].astype(F32)).astype(BF16)
         if p == 0:
             red.after("gated")
-            grad_ffn(1, d_gate)
-            red.after("gate")
-            grad_ffn(2, d_up)
-            red.after("up")
+            for wave, d, name in ((1, d_gate, "gate"), (2, d_up, "up")):
+                grad_ffn(wave, d, 0)
+                red.after(name + "_a")
+                grad_ffn(wave, d, 1)
+                red.after(name + "_b")
         dn[...] = nn(wg[...], d_gate[:, at]) + nn(wu[...], d_up[:, at])
         if p == 0:
             red.after("ffn")
@@ -509,20 +541,20 @@
                 ).astype(BF16)
             if p == 0:
                 red.after("scores_a" if first == 0 else "scores_b")
-        dn[...] = nn(wqkv[...], d_qkv[:, at])
+
+    def backward_end(p):
+        dn[...] = nn(wqkv[...], d_qkv[:, p * total : (p + 1) * total])
         if p == 0:
             red.after("qkv")
         norm_backward(p, x_of, 0, d_down.at[:, :total] if p == 1 else None)
-        if p == 0:
-            red.after("norm_one")
 
     forward(0)
     forward(1)
+    results = [pltpu.make_async_copy(out_ref, out_hbm, out_sem.at[0])]
+    results[0].start()
     backward(1)
+    backward_end(1)
     backward(0)
-    for i in range(2):
-        gain_buf[0, 0, i : i + 1, :D] = jnp.sum(gain_sum[i].T, axis=0, keepdims=True)
-    red.gain_step()
 
     column = lax.broadcasted_iota(jnp.int32, (1, CHUNK), 1)
     for c in range(3):
@@ -534,6 +566,13 @@
     for c in range(2):
         put(3 * TILES + 8 + 2 * c, nt(att[...], d_branch[c * CHUNK : (c + 1) * CHUNK, :]))
     red.after("rest")
+    backward_end(0)
+    results.append(pltpu.make_async_copy(dx_ref, dx_hbm, out_sem.at[1]))
+    results[1].start()
+    for i in range(2):
+        gain_buf[0, 0, i : i + 1, :D] = jnp.sum(gain_sum[i].T, axis=0, keepdims=True)
+    red.gain_step()
+    red.after("norm_one")
     red.after("end")
     while len(red.whole_gains) <= bits:
         red.gain_step()
@@ -541,6 +580,8 @@
     gain_out_ref[...] = jnp.where(core == 0, sums, pltpu.roll(sums, 640 - TILE_ROWS, 1))
     for copy in red.started:
         copy.wait_send()
+    for copy in results + red.leaving:
+        copy.wait()
 
 
 def run_layer(bits, lengths, tokens, cotangent, weights, gains):
@@ -553,7 +594,10 @@
     hbm = pl.BlockSpec(memory_space=pl.ANY)
     dma = pltpu.SemaphoreType.DMA
     grads = (WAVES * TILES, TILE_ROWS, 128)
+    table = jnp.asarray(rope_table())
     scratch = [
+        (tokens.shape, BF16), (tokens.shape, BF16), *((w.shape, BF16) for w in weights[:3]), (table.shape, BF16),
+        (tokens.shape, BF16), (tokens.shape, F32), (grads, BF16),
         ((D, QKV), BF16), ((D, D), BF16), ((D, FF), BF16), ((D, FF), BF16), ((D, FF), BF16),
         ((8, 640), F32), ((8, 640), F32), ((2, D, BUCKET), F32), ((2, D, BUCKET), F32),
         ((HD, total), F32), ((buckets, BUCKET, BUCKET), F32),
@@ -575,17 +619,17 @@
             jax.ShapeDtypeStruct(grads, BF16),
             jax.ShapeDtypeStruct((8, 640), F32),
         ),
-        in_specs=[pl.BlockSpec(memory_space=pltpu.SMEM)] + [vmem] * 5 + [hbm] * 4 + [vmem] * 3,
-        out_specs=(vmem,) * 4,
+        in_specs=[pl.BlockSpec(memory_space=pltpu.SMEM)] + [hbm] * 9 + [vmem] * 2 + [hbm],
+        out_specs=(hbm,) * 3 + (vmem,),
         scratch_shapes=[pltpu.VMEM(shape, dtype) for shape, dtype in scratch]
         + [
             dma((6,)), dma((6,)), dma((4,)), dma((WAVES,)), dma((WAVES,)), dma((slots, steps)),
-            dma((slots, steps)), dma((bits + 1,)), dma((bits + 1,)),
+            dma((slots, steps)), dma((bits + 1,)), dma((bits + 1,)), dma((slots,)), dma((6,)), dma((2,)),
         ],
         compiler_params=pltpu.CompilerParams(
             collective_id=0, has_side_effects=True, vmem_limit_bytes=63 << 20
         ),
-    )(lengths, tokens, cotangent, *weights, *gains, jnp.asarray(rope_table()))
+    )(lengths, tokens, cotangent, *weights, *gains, table)
 
 
 def unpack_kernel(

time: 109 us -> 103 us (0.945)
  Pallas kernels: 108 us -> 102 us
    pallas_call x1, Pallas kernels: 102 us -> 96 us  [run_layer(): pl.pallas_call(functools.partial(layer_kernel, bits, buckets), out_shape=...]
where the time goes in v1:
time: 103 us
  Pallas kernels  102 us (99%)
    pallas_call x1, Pallas kernels, run_layer(): pl.pallas_call(functools.partial(layer_kernel, bits, buckets), out_shape=...  96 us
    pallas_call x1, Pallas kernels, unpack(): pl.pallas_call(unpack_kernel, out_shape=(jax.ShapeDtypeStruct(output.shap...  6.25 us

profile of v1, /device:TPU:0, one launch (start us, length us, event | category | flops | bytes accessed | tf_op | source)
XLA Modules:
  0.0 103.1 jit_solution(217788879211064775)
XLA Ops:
  0.6 96.0 %shard_map.212 = (bf16[4,576,128]{2,1,0:T(8,128)(2,1)}, f32[4,576,128]{2,1,0:T(8,128)}, bf16[48,288,128]{2,1,0:T(8,128)(2,1)}, f32[8,640]{1,0:T(8,128)}) custom-call(s32[4,4]{1,0:T(4,128)} %bitcast.22, bf16[4,576,128]{2,1,0:T(8,128)(2,1)} %bitcast.20, bf16[4,576,128]{2,1,0:T(8,128)(2,1)} %bitcast.21, bf16[288,576]{1,0:T(8,128)(2,1)} %wq_hbm.1, ...), custom_call_target="tpu_custom_call" | custom-call | tf_op jit(solution)/shard_map/pallas_call | solution.py:614
  96.6 6.3 %shard_map.213 = (bf16[4,576,128]{2,1,0:T(8,128)(2,1)}, f32[4,576,128]{2,1,0:T(8,128)}, f32[288,576]{1,0:T(8,128)}, f32[288,192]{1,0:T(8,128)}, f32[288,192]{1,0...) custom-call(bf16[48,288,128]{2,1,0:T(8,128)(2,1)} %get-tuple-element, ...), custom_call_target="tpu_custom_call" | custom-call | tf_op jit(solution)/shard_map/pallas_call | solution.py:700

commit v2 on v1

--- a/solution.py
+++ b/solution.py
@@ -56,9 +56,9 @@
 
 
 STREAM_BITS = (
-    ((1, 2, 0), (0, 1, 2), (2, 1, 0)),
-    ((1, 0, 2), (0, 2, 1), (2, 1, 0)),
-    ((0, 2, 1), (1, 0, 2), (2, 1, 0)),
+    ((2, 1, 0), (0, 2, 1), (1, 0, 2)),
+    ((2, 0, 1), (0, 2, 1), (1, 0, 2)),
+    ((0, 1, 2), (2, 1, 0), (1, 2, 0)),
     ((2, 1, 0), (1, 0, 2), (0, 2, 1)),
 )
 
@@ -68,12 +68,12 @@
 
 
 TILE_TIME, STEP_TIME, WAVE_TIME, WAVE_STEP_TIME = 1.42, 2.65, 1.3, 1.5
-STEP_RANK, WAVE_RANK, THIRD_RANK = 6.404041155859943, 5.683458090508361, 0.024984608445357243
+STEP_RANK, WAVE_RANK, THIRD_RANK = 11.420752228273008, 10.744307844872964, -0.1535938302871354
 PARTS = (
-    ("down_a", 1.05, 0, 1.0), ("down_b", 1.05, None, 1.0), ("gated", 1.7, None, -1.0), ("gate_a", 1.05, None, -5.0),
-    ("gate_b", 1.05, 1, 0.0), ("up_a", 1.05, None, 1.0), ("up_b", 1.05, 2, 0.3), ("ffn", 2.1, None, 0.6),
-    ("norm_two", 0.75, None, -1.0), ("branch", 0.7, None, -5.0), ("scores_a", 1.0, None, 0.3),
-    ("scores_b", 1.0, None, 0.0), ("rest", 2.1, 3, 0.6), ("qkv", 0.85, None, 0.6), ("norm_one", 1.1, None, -1.0),
+    ("down_a", 1.05, 0, -5.0), ("down_b", 1.05, None, -5.0), ("gated", 1.7, None, 0.0), ("gate_a", 1.05, None, -1.0),
+    ("gate_b", 1.05, 1, 0.3), ("up_a", 1.05, None, 0.3), ("up_b", 1.05, 2, 0.6), ("ffn", 2.1, None, 1.0),
+    ("norm_two", 0.75, None, 0.0), ("branch", 0.7, None, -1.0), ("scores_a", 1.0, None, 0.6),
+    ("scores_b", 1.0, None, 0.3), ("rest", 2.1, 3, 0.6), ("qkv", 0.85, None, 0.6), ("norm_one", 1.1, None, 0.0),
     ("end", 0.0, None, 1e9),
 )
 
@@ -182,7 +182,7 @@
                 self.halves[w].wait()
             self.stream_step(w, s, step)
             self.count += 1
-            if name == "end" and self.count % 8 == 0:
+            if name == "end" and self.count % 11 == 0:
                 self.gain_step()
 
     def gain_step(self):

time: 103 us -> 103 us (level)
  no operation moved by 1% of the time
where the time goes in v2:
time: 103 us
  Pallas kernels  102 us (99%)
    pallas_call x1, Pallas kernels, run_layer(): pl.pallas_call(functools.partial(layer_kernel, bits, buckets), out_shape=...  96.1 us
    pallas_call x1, Pallas kernels, unpack(): pl.pallas_call(unpack_kernel, out_shape=(jax.ShapeDtypeStruct(output.shap...  6.25 us

profile of v2, /device:TPU:0, one launch (start us, length us, event | category | flops | bytes accessed | tf_op | source)
XLA Modules:
  0.0 103.2 jit_solution(10416713469253744709)
XLA Ops:
  0.6 96.1 %shard_map.212 = (bf16[4,576,128]{2,1,0:T(8,128)(2,1)}, f32[4,576,128]{2,1,0:T(8,128)}, bf16[48,288,128]{2,1,0:T(8,128)(2,1)}, f32[8,640]{1,0:T(8,128)}) custom-call(s32[4,4]{1,0:T(4,128)} %bitcast.22, bf16[4,576,128]{2,1,0:T(8,128)(2,1)} %bitcast.20, bf16[4,576,128]{2,1,0:T(8,128)(2,1)} %bitcast.21, bf16[288,576]{1,0:T(8,128)(2,1)} %wq_hbm.1, ...), custom_call_target="tpu_custom_call" | custom-call | tf_op jit(solution)/shard_map/pallas_call | solution.py:614
  96.8 6.3 %shard_map.213 = (bf16[4,576,128]{2,1,0:T(8,128)(2,1)}, f32[4,576,128]{2,1,0:T(8,128)}, f32[288,576]{1,0:T(8,128)}, f32[288,192]{1,0:T(8,128)}, f32[288,192]{1,0...) custom-call(bf16[48,288,128]{2,1,0:T(8,128)(2,1)} %get-tuple-element, ...), custom_call_target="tpu_custom_call" | custom-call | tf_op jit(solution)/shard_map/pallas_call | solution.py:700
